TPU v7x, 32 devices: a whole 2x2x4 slice. The times are simulated.
32 devices in a mesh: ctx: 16 (over z, y, x), head: 2 (over core).
Axes of the slice: x: 2, y: 2, z: 4, core: 2. Of those that a mesh axis runs over, the one named last changes fastest.
Arguments:
- tokens: bfloat16 [4096, 2048], P('ctx', 'head'), may hold values from -6 to 6
- qkv_weight: bfloat16 [2048, 3, 2048], P('ctx', None, 'head'), may hold values from -0.125 to 0.125
- out_gain: float32 [2048], P('head'), may hold values from 0.1 to 1.9
Outputs:
- attended: bfloat16 [4096, 2048], P('ctx', 'head')
All inputs are finite; a program needn't handle non-finite values.
Results may differ from a plain program's by a relative error of at most 0.001.
Values may be sent and summed in bfloat16 or wider, within the bound.
A program may use at most 64 MiB of HBM per device.

v0:
```python
import math

import jax
import jax.numpy as jnp
from jax import lax
from jax.sharding import PartitionSpec as P

HD = 128


epsilon = 1e-06
highest = lax.Precision.HIGHEST


def prefix(x, axis, combine, identity):
    peers, here = (lax.axis_size(axis), lax.axis_index(axis))
    everything = jax.tree.map(lambda part: lax.all_gather(part, axis), x)
    start = jax.tree.map(
        lambda part, zero: jnp.broadcast_to(jnp.asarray(zero, part.dtype), part.shape), x, identity
    )

    def step(k, before):
        reached = k < here
        new = combine(before, jax.tree.map(lambda part: part[k], everything))
        return jax.tree.map(lambda a, b: jnp.where(reached, a, b), new, before)

    return lax.fori_loop(0, peers, step, start)


def matmul_heads(left_mat, right_mat):
    return jnp.einsum("hij,hjk->hik", left_mat, right_mat, precision=highest)


def block_terms(queries, key_rows, val_rows, prior_s, prior_m):
    rows_here = queries.shape[0]
    row_ids = lax.broadcasted_iota(jnp.int32, (rows_here, rows_here), 0)
    col_ids = lax.broadcasted_iota(jnp.int32, (rows_here, rows_here), 1)
    causal = row_ids >= col_ids
    strict = row_ids < col_ids
    scores = jnp.einsum("thd,shd->hts", queries, key_rows, precision=highest)
    lower_part = jnp.where(causal, scores, 0.0)
    pair_term = jnp.einsum("hti,hji->htj", lower_part, lower_part, precision=highest)
    query_state = jnp.einsum("thd,hde->the", queries, prior_s, precision=highest)
    cross_term = jnp.einsum("the,she->hts", query_state, queries, precision=highest)
    mixing = jnp.where(causal, pair_term + cross_term, 0.0)
    raw_out = jnp.einsum("hts,she->the", mixing, val_rows, precision=highest)
    raw_out = raw_out + jnp.einsum("thd,hde->the", queries, prior_m, precision=highest)
    local_s = jnp.einsum("thd,the->hde", key_rows, key_rows, precision=highest)
    local_c = jnp.einsum("thd,the->hde", queries, val_rows, precision=highest)
    upper_part = jnp.where(strict, scores, 0.0)
    weighted = jnp.einsum("hji,jhe->ihe", upper_part, val_rows, precision=highest)
    local_g = jnp.einsum("ihd,ihe->hde", key_rows, weighted, precision=highest)
    return (raw_out, local_s, local_c, local_g)


def combine_pairs(earlier, later_part):
    return (earlier[0] + later_part[0], earlier[1] + later_part[1])


def combine_single(earlier, later_part):
    return earlier + later_part


def body(tokens, qkv_weight, out_gain):
    gathered = lax.all_gather(tokens, "head", axis=1, tiled=True)
    rows_here = gathered.shape[0]
    col_count = qkv_weight.shape[2]
    head_count = col_count // HD
    projected = jnp.einsum(
        "tr,rch->cth",
        gathered,
        lax.all_gather(qkv_weight, "ctx", axis=0, tiled=True),
        preferred_element_type=jnp.float32,
    )
    block_len = math.gcd(rows_here, 128)
    block_count = rows_here // block_len
    projected = projected.reshape(3, block_count, block_len, head_count, HD)
    queries = projected[0]
    key_rows = projected[1]
    val_rows = projected[2]
    zeros_state = jnp.zeros((head_count, HD, HD), jnp.float32)

    def local_step(carry, pieces):
        run_s, run_c, run_g = carry
        query_blk, key_blk, val_blk = pieces
        run_m = matmul_heads(run_s, run_c) - run_g
        raw_blk, add_s, add_c, add_g = block_terms(query_blk, key_blk, val_blk, run_s, run_m)
        next_g = run_g + add_g + matmul_heads(add_s, run_c)
        return ((run_s + add_s, run_c + add_c, next_g), (raw_blk, run_c))

    totals, outputs = lax.scan(
        local_step, (zeros_state, zeros_state, zeros_state), (queries, key_rows, val_rows)
    )
    local_s, local_c, local_g = totals
    local_raw, before_c = outputs
    prior_s, prior_c = prefix((local_s, local_c), "ctx", combine_pairs, (zeros_state, zeros_state))
    own_term = local_g + matmul_heads(local_s, prior_c)
    prior_g = prefix(own_term, "ctx", combine_single, zeros_state)
    prior_m = matmul_heads(prior_s, prior_c) - prior_g
    row_ids = lax.broadcasted_iota(jnp.int32, (block_len, block_len), 0)
    col_ids = lax.broadcasted_iota(jnp.int32, (block_len, block_len), 1)
    causal = row_ids >= col_ids
    query_state = jnp.einsum("bthd,hde->bthe", queries, prior_s, precision=highest)
    cross_scores = jnp.einsum("bthe,bshe->bhts", query_state, queries, precision=highest)
    cross_scores = jnp.where(causal, cross_scores, 0.0)
    extra = jnp.einsum("bhts,bshe->bthe", cross_scores, val_rows, precision=highest)
    extra = extra + jnp.einsum("bthd,bhde->bthe", query_state, before_c, precision=highest)
    extra = extra + jnp.einsum("bthd,hde->bthe", queries, prior_m, precision=highest)
    raw_out = (local_raw + extra).reshape(rows_here, head_count, HD)
    mean_sq = jnp.mean(raw_out * raw_out, axis=-1, keepdims=True)
    normed = raw_out * lax.rsqrt(mean_sq + epsilon) * out_gain.reshape(head_count, HD)
    return normed.reshape(rows_here, col_count).astype(jnp.bfloat16)


def solution(mesh):
    in_specs = (P("ctx", "head"), P("ctx", None, "head"), P("head"))
    out_specs = P("ctx", "head")
    return jax.shard_map(body, mesh=mesh, in_specs=in_specs, out_specs=out_specs, check_vma=False)
```

profile of v0, /device:TPU:25, one launch (start us, length us, event | category | flops | bytes accessed | tf_op | source)
XLA Modules:
  0.0 663.9 jit_solution(9046018835466905909)
XLA Ops:
  7.3 2.3 copy.75
  9.7 10.0 %all-gather.11.cloned.1.call-done = bf16[256,2048]{1,0:T(8,128)(2,1)} async-done(((bf16[256,1024]{1,0:T(8,128)(2,1)}), bf16[256,2048]{1,0:T(8,128)(2,1)}) %all-gather.11.cloned.1.call-update) | async-done | bytes 1048592 | tf_op jit(solution)/shard_map/all_gather | solution.py:65
  19.7 197.4 %all-gather.9.cloned.1.call-done = bf16[2048,3,1024]{0,2,1:T(8,128)(2,1)} async-done(((bf16[128,3,1024]{0,2,1:T(8,128)(2,1)}), bf16[2048,3,1024]{0,2,1:T(8,128)(2,1)}) %all-gather.9.cloned.1.call-update) | async-done | bytes 12582928 | tf_op jit(solution)/shard_map/all_gather | solution.py:72
  217.1 6.9 %convolution_bitcast_fusion.2 = f32[3,256,1024]{1,2,0:T(8,128)S(1)} fusion(bf16[2048,3,1024]{0,2,1:T(8,128)(2,1)} %all-gather.9.cloned.1.call-done, bf16[256,2048]{1,0:T(8,128)(2,1)} %all-gather.11.cloned.1.call-done), kind=kOutput, calls=%fused_computation.43 | convolution fusion | flops 3221225472 | bytes 16777216 | tf_op jit(solution)/shard_map/tr,rch->cth/dot_general | solution.py:69
  225.6 2.7 squeeze.41
  228.3 2.7 squeeze.42
  232.5 33.3 %while.52 = (s32[]{:T(128)}, f32[8,128,128]{2,1,0:T(8,128)S(1)}, f32[8,128,128]{2,1,0:T(8,128)S(1)}, f32[8,128,128]{2,1,0:T(8,128)S(1)}, f32[2,128,8,128]{1,3,2,...) while((s32[]{:T(128)}, f32[8,128,128]{2,1,0:T(8,128)S(1)}, ...), condition=%wide.region_1.2_spmd.clone.clone, body=%wide.region_0.1_spmd.clone.sunk.clone | while | flops 2418442240 | bytes 43073768 | solution.py:91
  232.5 2.6 constant_dynamic-slice_fusion.8
  236.1 1.8 constant_dynamic-slice_fusion.7
  249.1 2.6 constant_dynamic-slice_fusion.8
  252.8 1.8 constant_dynamic-slice_fusion.7
  267.3 110.5 %all-gather.13.cloned.1.call-done = f32[128,128,128]{2,1,0:T(8,128)} async-done(((f32[8,128,128]{2,1,0:T(8,128)}), f32[128,128,128]{2,1,0:T(8,128)}) %all-gather.13.cloned.1.call-update) | async-done | bytes 8388624 | tf_op jit(solution)/shard_map/all_gather | solution.py:17
  377.8 113.7 %all-gather.15.cloned.1.call-done = f32[128,128,128]{2,1,0:T(8,128)} async-done(((f32[8,128,128]{2,1,0:T(8,128)}), f32[128,128,128]{2,1,0:T(8,128)}) %all-gather.15.cloned.1.call-update) | async-done | bytes 8388624 | tf_op jit(solution)/shard_map/all_gather | solution.py:17
  491.4 25.4 %while.53 = (s32[]{:T(128)}, f32[8,128,128]{2,1,0:T(8,128)S(1)}, f32[8,128,128]{2,1,0:T(8,128)S(1)}, s32[]{:T(128)}, f32[16,8,128,128]{3,2,1,0:T(8,128)}, /*index=5*/f32[16,8,128,128]{3,2,1,0:T(8,128)}) while((s32[]{:T(128)}, f32[8,128,128]{2,1,0:T(8,128)S(1)}, f32[8,128,128]{2,1,0:T(8,128)S(1)}, s32[]{:T(128)}, ...), condition=%wide.region_3.4_spmd.clone.clone, body=%wide.region_2.3_spmd.clone.sunk.clone | while | flops 786436 | bytes 3145821 | solution.py:27
  491.4 1.6 add_select_fusion.7
  493.1 1.6 add_select_fusion.7
  494.7 1.6 add_select_fusion.7
  496.3 1.6 add_select_fusion.7
  497.9 1.6 add_select_fusion.7
  499.4 1.6 add_select_fusion.7
  501.0 1.6 add_select_fusion.7
  502.6 1.6 add_select_fusion.7
  504.2 1.6 add_select_fusion.7
  505.8 1.6 add_select_fusion.7
  507.4 1.6 add_select_fusion.7
  508.9 1.6 add_select_fusion.7
  510.5 1.6 add_select_fusion.7
  521.7 3.3 convolution_select_fusion
  525.0 4.6 fusion.32
  529.6 99.9 %all-gather.17.cloned.1.call-done = f32[128,128,128]{2,1,0:T(8,128)} async-done(((f32[8,128,128]{2,1,0:T(8,128)}), f32[128,128,128]{2,1,0:T(8,128)}) %all-gather.17.cloned.1.call-update) | async-done | bytes 8388624 | tf_op jit(solution)/shard_map/all_gather | solution.py:17
  629.5 20.0 %while.54 = (s32[]{:T(128)}, f32[8,128,128]{2,1,0:T(8,128)S(1)}, s32[]{:T(128)}, f32[16,8,128,128]{3,2,1,0:T(8,128)}) while((s32[]{:T(128)}, f32[8,128,128]{2,1,0:T(8,128)S(1)}, s32[]{:T(128)}, f32[16,8,128,128]{3,2,1,0:T(8,128)}) %tuple.125), condition=%wide.region_5.6_spmd.clone.clone, body=%wide.region_4.5_spmd.clone.sunk.clone | while | flops 393220 | bytes 1572941 | solution.py:27
  651.3 4.1 multiply_reduce_fusion
  (110 shorter events, 62.2 us)
Async XLA Ops:
  6.5 13.1 %all-gather.11.cloned.1.call-start = ((), (), s32[]{:S(2)}) async-start(), calls=%async_computation.1 | async-start | bytes 1572864 | tf_op jit(solution)/shard_map/all_gather | solution.py:65
  7.3 209.8 %all-gather.9.cloned.1.call-start = ((), (), s32[]{:S(2)}) async-start(), calls=%async_computation | async-start | bytes 13369344 | tf_op jit(solution)/shard_map/all_gather | solution.py:72
  9.6 368.2 %all-gather.13.cloned.1.call-start = ((), (), s32[]{:S(2)}) async-start(), calls=%async_computation.2 | async-start | bytes 8912896 | tf_op jit(solution)/shard_map/all_gather | solution.py:17
  235.1 7.6 %copy-start.6 = (f32[2,128,8,128]{1,3,2,0:T(8,128)S(1)}, f32[2,128,8,128]{1,3,2,0:T(8,128)}, u32[]{:S(2)}) copy-start(f32[2,128,8,128]{1,3,2,0:T(8,128)} %get-tuple-element.599) | copy-start | bytes 3145732 | tf_op jit(solution)/shard_map/while
  240.2 7.5 %copy-start.8 = (f32[2,8,128,128]{3,2,1,0:T(8,128)S(1)}, f32[2,8,128,128]{3,2,1,0:T(8,128)}, u32[]{:S(2)}) copy-start(f32[2,8,128,128]{3,2,1,0:T(8,128)} %get-tuple-element.600) | copy-start | bytes 3145732 | tf_op jit(solution)/shard_map/while
  243.8 5.3 copy-start.7
  247.8 1.3 copy-start.9
  251.8 7.6 %copy-start.6 = (f32[2,128,8,128]{1,3,2,0:T(8,128)S(1)}, f32[2,128,8,128]{1,3,2,0:T(8,128)}, u32[]{:S(2)}) copy-start(f32[2,128,8,128]{1,3,2,0:T(8,128)} %get-tuple-element.599) | copy-start | bytes 3145732 | tf_op jit(solution)/shard_map/while
  256.8 7.5 %copy-start.8 = (f32[2,8,128,128]{3,2,1,0:T(8,128)S(1)}, f32[2,8,128,128]{3,2,1,0:T(8,128)}, u32[]{:S(2)}) copy-start(f32[2,8,128,128]{3,2,1,0:T(8,128)} %get-tuple-element.600) | copy-start | bytes 3145732 | tf_op jit(solution)/shard_map/while
  260.4 5.3 copy-start.7
  264.4 1.3 copy-start.9
  265.8 0.8 copy-start.1
  265.8 1.0 copy-start
  266.6 250.3 %copy-start.2 = (f32[8,128,128]{2,1,0:T(8,128)S(1)}, f32[8,128,128]{2,1,0:T(8,128)}, u32[]{:S(2)}) copy-start(f32[8,128,128]{2,1,0:T(8,128)} %copy-done.1) | copy-start | bytes 1572868
  266.6 224.8 %all-gather.15.cloned.1.call-start = ((), (), s32[]{:S(2)}) async-start(), calls=%async_computation.3 | async-start | bytes 8912896 | tf_op jit(solution)/shard_map/all_gather | solution.py:17
  267.2 362.3 %all-gather.17.cloned.1.call-start = ((), (), s32[]{:S(2)}) async-start(), calls=%async_computation.4 | async-start | bytes 8912896 | tf_op jit(solution)/shard_map/all_gather | solution.py:17
  491.4 26.9 %copy-start.3 = (f32[2,128,8,128]{1,0,3,2:T(2,128)S(1)}, f32[2,128,8,128]{1,0,3,2:T(2,128)}, u32[]{:S(2)}) copy-start(f32[2,128,8,128]{1,0,3,2:T(2,128)} %get-tuple-element.652) | copy-start | bytes 3145732
  520.7 1.0 copy-start.5
  521.7 128.4 %copy-start.4 = (f32[2,128,8,128]{3,1,2,0:T(8,128)S(1)}, f32[2,128,8,128]{3,1,2,0:T(8,128)}, u32[]{:S(2)}) copy-start(f32[2,128,8,128]{3,1,2,0:T(8,128)} %copy.82) | copy-start | bytes 3145732
  649.5 6.7 %copy-start.10 = (f32[1024]{0:T(1024)S(1)}, f32[1024]{0:T(1024)}, u32[]{:S(2)}) copy-start(f32[1024]{0:T(1024)} %param.11) | copy-start | bytes 12292
Sparse Core Ops, SparseCore 0:
  8.9 10.7 all-gather.10
  22.4 194.6 all-gather.8
  266.7 110.9 all-gather.12
  380.4 111.0 all-gather.14
  518.5 111.0 all-gather.16
where the time goes:
time: 669 us; the launch traced here: 664 us
  waiting for transfers between devices  533 us (80%)
  matrix products  46.9 us (7%)
  other arithmetic  46 us (7%)
  local copies, waits for them, and re-layouts  23.7 us (4%)
  between operations  13.4 us (2%)
    all_gather x3, waiting for transfers between devices, prefix(): everything = jax.tree.map(lambda part: lax.all_gather(part, axis), x)  324 us
    all_gather x1, waiting for transfers between devices, body(): lax.all_gather(qkv_weight, 'ctx', axis=0, tiled=True)  197 us
    select_n x32, other arithmetic, step(): return jax.tree.map(lambda a, b: jnp.where(reached, a, b), new, before)  44.7 us
  transfers between devices with their start and end apart: 5, of which 5 were waited for; matrix products, arithmetic and copies ran while one was open for 2% of the time, Pallas kernels for 0%

commit v1 on v0

v1 whole, which is shorter than its diff:
```python
import functools
import math

import jax
import jax.numpy as jnp
from jax import lax
from jax.experimental import pallas as pl
from jax.experimental.pallas import tpu as pltpu
from jax.sharding import PartitionSpec as P

HD = 128
GROUP = 4
BLOCK = 256

epsilon = 1e-06
MESH = pl.DeviceIdType.MESH
NN = (((1,), (0,)), ((), ()))
NT = (((1,), (1,)), ((), ()))
TN = (((0,), (0,)), ((), ()))


def split(x):
    high = x.astype(jnp.bfloat16)
    low = (x - high.astype(jnp.float32)).astype(jnp.bfloat16)
    return high, low


def dot(a, b, dims):
    one = functools.partial(
        lax.dot_general, dimension_numbers=dims, preferred_element_type=jnp.float32
    )
    return one(a[0], b[0]) + (one(a[0], b[1]) + one(a[1], b[0]))


def kernel(
    n, peers, group, x_ref, w_ref, gain_ref, out_ref,
    xbuf, wbuf, proj, ubuf, raw, s_own, s_in, r_own, r_in, state, result, landed,
    own_sem, wrecv, wa_send, wup, wdown, xrecv, xsend, xcore, ssend, srecv, rsend, rrecv, osend, orecv,
):
    me, e = lax.axis_index("ctx"), lax.axis_index("head")
    t, h = me // group, me % group
    turns = n // group
    toks, feats = x_ref.shape
    rows = w_ref.shape[1]
    width = wbuf.shape[2]
    heads = width // HD
    total = toks * group

    def ring(j):
        return (h + j) % group

    def other(o):
        return (e + o) % peers

    def at(tt, hh):
        return tt * group + hh

    barrier = pltpu.get_barrier_semaphore()
    for j in range(1, group):
        pl.semaphore_signal(barrier, inc=1, device_id=(at(t, ring(j)), e), device_id_type=MESH)
    for o in range(1, peers):
        pl.semaphore_signal(barrier, inc=1, device_id=(me, other(o)), device_id_type=MESH)

    @pl.loop(1, turns)
    def _(k):
        pl.semaphore_signal(
            barrier, inc=1, device_id=(at((t + k) % turns, h), e), device_id_type=MESH
        )

    pl.semaphore_wait(barrier, group - 1 + peers - 1 + turns - 1)

    def remote(src, dst, send, recv, to):
        return pltpu.make_async_remote_copy(
            src_ref=src, dst_ref=dst, send_sem=send, recv_sem=recv, device_id=to, device_id_type=MESH
        )

    def columns(hh):
        return pl.ds(pl.multiple_of(hh * width, width), width)

    def slot(s):
        return wbuf.at[:, pl.ds(pl.multiple_of(s * rows, rows), rows), :]

    def tok(hh):
        return pl.ds(pl.multiple_of(hh * toks, toks), toks)

    def xslot(hh, ee):
        return xbuf.at[tok(hh), pl.ds(pl.multiple_of(ee * feats, feats), feats)]

    def up(s):
        return remote(slot(s), slot(s), wup.at[s], wrecv.at[s], (at((t + 1) % turns, h), e))

    def down(s):
        return remote(
            slot(s), slot(s), wdown.at[s], wrecv.at[s], (at((t + turns - 1) % turns, h), e)
        )

    def across(j):
        hp = ring(j)
        return remote(w_ref.at[:, :, columns(hp)], slot(me), wa_send.at[j], wrecv.at[me], (at(t, hp), e))

    def xacross(j):
        return remote(x_ref, xslot(h, e), xsend.at[j], xrecv.at[h, e], (at(t, ring(j)), e))

    def xsibling(j, o):
        hs = ring(j)
        src = x_ref if j == 0 else xslot(hs, e)
        return remote(src, xslot(hs, e), xcore.at[j, o], xrecv.at[hs, e], (me, other(o)))

    w_own = pltpu.make_async_copy(w_ref.at[:, :, columns(h)], slot(me), own_sem.at[0])
    x_own = pltpu.make_async_copy(x_ref, xslot(h, e), own_sem.at[1])
    w_own.start()
    for j in range(1, group):
        across(j).start()
    x_own.start()
    w_own.wait()

    def send_up(s):
        @pl.when(t + 1 < turns)
        def _():
            up(s).start()

    def send_down(s):
        @pl.when(t > 0)
        def _():
            down(s).start()

    send_up(me)
    send_down(me)
    for j in range(1, group):
        xacross(j).start()
    for o in range(1, peers):
        xsibling(0, o).start()
    for j in range(1, group):
        s = at(t, ring(j))
        up(s).wait_recv()
        send_up(s)
        send_down(s)

    def arrive(d):
        for j in range(group):
            @pl.when(t - d >= 0)
            def _():
                s = at(t - d, ring(j))
                up(s).wait_recv()
                send_up(s)

            @pl.when(t + d < turns)
            def _():
                s = at(t + d, ring(j))
                down(s).wait_recv()
                send_down(s)

    first = min(2, turns)
    for d in range(1, first):
        arrive(d)

    x_own.wait()
    for j in range(1, group):
        remote(x_ref, xslot(ring(j), e), xsend.at[j], xrecv.at[ring(j), e], (me, other(1))).wait_recv()
        for o in range(1, peers):
            xsibling(j, o).start()
    for j in range(group):
        for o in range(1, peers):
            remote(
                x_ref, xslot(ring(j), other(o)), xcore.at[j, o], xrecv.at[ring(j), other(o)], (me, other(o))
            ).wait_recv()

    depth = rows * group

    def multiply(ts, fresh):
        ks = pl.ds(pl.multiple_of(ts * depth, depth), depth)

        @pl.loop(0, group)
        def _(m):
            block = xbuf[tok(m), ks]
            for c in range(3):
                part = lax.dot_general(
                    block, wbuf[c, ks, :], NN, preferred_element_type=jnp.float32
                )
                if fresh:
                    proj[c, tok(m), :] = part
                else:
                    proj[c, tok(m), :] += part

    def multiply_at(d):
        @pl.when(t - d >= 0)
        def _():
            multiply(t - d, False)

        @pl.when(t + d < turns)
        def _():
            multiply(t + d, False)

    if depth % 128 == 0:
        multiply(t, True)
        for d in range(1, first):
            multiply_at(d)

        @pl.loop(first, turns)
        def _(d):
            arrive(d)
            multiply_at(d)
    else:
        @pl.loop(first, turns)
        def _(d):
            arrive(d)

        @pl.loop(0, group)
        def _(m):
            for c in range(3):
                proj[c, tok(m), :] = lax.dot_general(
                    xbuf[tok(m), :], wbuf[c], NN, preferred_element_type=jnp.float32
                )

    blk = math.gcd(total, BLOCK)
    blocks = total // blk
    causal = lax.broadcasted_iota(jnp.int32, (blk, blk), 0) >= lax.broadcasted_iota(
        jnp.int32, (blk, blk), 1
    )

    def part(c, b, i):
        return split(proj[c, pl.ds(pl.multiple_of(b * blk, blk), blk), i * HD : (i + 1) * HD])

    def span(b):
        return pl.ds(pl.multiple_of(b * blk, blk), blk)

    def hcols(i):
        return slice(i * HD, (i + 1) * HD)

    def push(own, into, send, recv):
        def copy(tp):
            return remote(own, into.at[t], send.at[tp], recv.at[t], (at(tp, h), e))
        return copy

    s_push = push(s_own, s_in, ssend, srecv)
    r_push = push(r_own, r_in, rsend, rrecv)

    s_own[...] = jnp.zeros_like(s_own)

    @pl.loop(0, blocks)
    def _(b):
        for i in range(heads):
            keys = part(1, b, i)
            s_own[i] += dot(keys, keys, TN)

    @pl.loop(t + 1, turns)
    def _(tp):
        s_push(tp).start()

    state[...] = jnp.zeros_like(state)

    @pl.loop(0, blocks)
    def _(b):
        for i in range(heads):
            q, k = part(0, b, i), part(1, b, i)
            scores = jnp.where(causal, dot(q, k, NT), 0.0)
            ubuf[span(b), hcols(i)] = dot(split(scores), k, NN) + dot(q, split(state[i]), NN)
            state[i] += dot(k, k, TN)

    def earlier(own, into, recv):
        state[...] = jnp.zeros_like(state)

        @pl.loop(0, t)
        def _(ts):
            remote(own, into.at[ts], ssend.at[0], recv.at[ts], (at((t + 1) % turns, h), e)).wait_recv()
            state[...] += into[ts]

    earlier(s_own, s_in, srecv)
    r_own[...] = jnp.zeros_like(r_own)

    @pl.loop(0, blocks)
    def _(b):
        for i in range(heads):
            u = ubuf[span(b), hcols(i)] + dot(part(0, b, i), split(state[i]), NN)
            ubuf[span(b), hcols(i)] = u
            r_own[i] += dot(split(u), part(2, b, i), TN)

    @pl.loop(t + 1, turns)
    def _(tp):
        r_push(tp).start()

    state[...] = jnp.zeros_like(state)

    @pl.loop(0, blocks)
    def _(b):
        for i in range(heads):
            q, v = part(0, b, i), part(2, b, i)
            u = split(ubuf[span(b), hcols(i)])
            scores = jnp.where(causal, dot(q, u, NT), 0.0)
            raw[span(b), hcols(i)] = dot(split(scores), v, NN) + dot(q, split(state[i]), NN)
            state[i] += dot(u, v, TN)

    earlier(r_own, r_in, rrecv)

    def give(j):
        hp = ring(j)
        return remote(
            result.at[tok(hp), :], landed.at[:, columns(h)], osend.at[j], orecv.at[h], (at(t, hp), e)
        )

    for j in list(range(1, group)) + [0]:
        rs = tok(ring(j))
        for i in range(heads):
            full = raw[rs, hcols(i)] + dot(split(proj[0, rs, hcols(i)]), split(state[i]), NN)
            mean_sq = jnp.mean(full * full, axis=-1, keepdims=True)
            gain = gain_ref[:, pl.ds(pl.multiple_of(h * width + i * HD, HD), HD)]
            result[rs, hcols(i)] = (full * lax.rsqrt(mean_sq + epsilon) * gain).astype(jnp.bfloat16)
        if j:
            give(j).start()
    o_own = pltpu.make_async_copy(result.at[tok(h), :], landed.at[:, columns(h)], own_sem.at[2])
    o_own.start()

    for j in range(1, group):
        across(j).wait_send()
        xacross(j).wait_send()
    for j in range(group):
        for o in range(1, peers):
            xsibling(j, o).wait_send()

    @pl.when(t + 1 < turns)
    def _():
        @pl.loop(0, at(t + 1, 0))
        def _(s):
            up(s).wait_send()

    @pl.when(t > 0)
    def _():
        @pl.loop(at(t, 0), n)
        def _(s):
            down(s).wait_send()

    @pl.loop(t + 1, turns)
    def _(tp):
        s_push(tp).wait_send()
        r_push(tp).wait_send()

    o_own.wait()
    for j in range(1, group):
        give(j).wait_send()
        hs = ring(j)
        remote(
            result.at[tok(h), :], landed.at[:, columns(hs)], osend.at[j], orecv.at[hs], (at(t, hs), e)
        ).wait_recv()
    out_ref[...] = landed[...]


def body(tokens, qkv_weight, out_gain):
    n, peers = lax.axis_size("ctx"), lax.axis_size("head")
    toks, feats = tokens.shape
    rows, _, cols = qkv_weight.shape
    group = math.gcd(math.gcd(n, cols // HD), GROUP)
    turns = n // group
    width = cols // group
    heads = width // HD
    total = toks * group
    moments = (heads, HD, HD)
    f32, bf16 = jnp.float32, jnp.bfloat16
    dma = pltpu.SemaphoreType.DMA
    vmem = pl.BlockSpec(memory_space=pltpu.VMEM)
    return pl.pallas_call(
        functools.partial(kernel, n, peers, group),
        out_shape=jax.ShapeDtypeStruct((toks, cols), bf16),
        in_specs=[vmem] * 3,
        out_specs=vmem,
        scratch_shapes=[
            pltpu.VMEM((total, feats * peers), bf16),
            pltpu.VMEM((3, rows * n, width), bf16),
            pltpu.VMEM((3, total, width), f32),
            pltpu.VMEM((total, width), f32),
            pltpu.VMEM((total, width), f32),
            pltpu.VMEM(moments, f32),
            pltpu.VMEM((turns,) + moments, f32),
            pltpu.VMEM(moments, f32),
            pltpu.VMEM((turns,) + moments, f32),
            pltpu.VMEM(moments, f32),
            pltpu.VMEM((total, width), bf16),
            pltpu.VMEM((toks, cols), bf16),
            dma((3,)),
            dma((n,)),
            dma((group,)),
            dma((n,)),
            dma((n,)),
            dma((group, peers)),
            dma((group,)),
            dma((group, peers)),
            dma((turns,)),
            dma((turns,)),
            dma((turns,)),
            dma((turns,)),
            dma((group,)),
            dma((group,)),
        ],
        compiler_params=pltpu.CompilerParams(
            collective_id=0, has_side_effects=True, vmem_limit_bytes=48 * 1024 * 1024
        ),
    )(tokens, qkv_weight.transpose(1, 0, 2), out_gain.reshape(1, cols))


def solution(mesh):
    in_specs = (P("ctx", "head"), P("ctx", None, "head"), P("head"))
    out_specs = P("ctx", "head")
    return jax.shard_map(body, mesh=mesh, in_specs=in_specs, out_specs=out_specs, check_vma=False)
```

time: 669 us -> 98.5 us (0.15)
  waiting for transfers between devices: 533 us -> 0 us
  Pallas kernels: 0 us -> 94.6 us
  matrix products: 46.9 us -> 0 us
  other arithmetic: 46 us -> 0 us
  local copies, waits for them, and re-layouts: 23.7 us -> 3.66 us
  between operations: 13.4 us -> 0.01 us
    all_gather x5 -> x0, waiting for transfers between devices: 532 us -> none  [the longest x3 324 us: prefix(): everything = jax.tree.map(lambda part: lax.all_gather(part, axis), x)]
    pallas_call x0 -> x1, Pallas kernels: none -> 94.6 us  [body(): pl.pallas_call(functools.partial(kernel, n, peers, group), out_shape=jax....]
    dot_general x32 -> x0, matrix products: 46.9 us -> none  [the longest x1 6.89 us: body(): jnp.einsum('tr,rch->cth', gathered, lax.all_gather(qkv_weight, 'ctx', axi...]
    select_n x32 -> x0, other arithmetic: 44.7 us -> none  [step(): return jax.tree.map(lambda a, b: jnp.where(reached, a, b), new, before)]
    dynamic_slice x4 -> x0, local copies, waits for them, and re-layouts: 8.8 us -> none  [body(): lax.scan(local_step, (zeros_state, zeros_state, zeros_state), (queries, k...]
    squeeze x4 -> x0, local copies, waits for them, and re-layouts: 8.24 us -> none  [the longest x2 4.01 us: body(): queries = projected[0]]
  transfers between devices with their start and end apart: 5 -> 0, of which waited for: 5 -> 0; matrix products, arithmetic and copies ran while one was open for 2% -> 0% of each run, Pallas kernels for 0% -> 0%
where the time goes in v1:
time: 98.5 us; the launch traced here: 98.3 us
  Pallas kernels  94.6 us (96%)
  local copies, waits for them, and re-layouts  3.66 us (4%)
    pallas_call x1, Pallas kernels, body(): pl.pallas_call(functools.partial(kernel, n, peers, group), out_shape=jax....  94.6 us
    unnamed x7, local copies, waits for them, and re-layouts  3.66 us

profile of v1, /device:TPU:25, one launch (start us, length us, event | category | flops | bytes accessed | tf_op | source)
XLA Modules:
  0.0 98.3 jit_solution(6185488261265246924)
XLA Ops:
  0.0 0.0 copy-start
  0.0 1.1 %copy-done = bf16[128,3,1024]{2,0,1:T(8,128)(2,1)S(1)} copy-done((bf16[128,3,1024]{2,0,1:T(8,128)(2,1)S(1)}, bf16[128,3,1024]{2,0,1:T(8,128)(2,1)}, u32[]{:S(2)}) %copy-start) | copy-done | bytes 786456
  1.1 0.0 copy-start.1
  1.1 1.0 %copy-done.1 = bf16[256,1024]{1,0:T(8,128)(2,1)S(1)} copy-done((bf16[256,1024]{1,0:T(8,128)(2,1)S(1)}, bf16[256,1024]{1,0:T(8,128)(2,1)}, u32[]{:S(2)}) %copy-start.1) | copy-done | bytes 524312
  2.2 0.0 copy-start.2
  2.2 0.7 copy-done.2
  2.9 94.6 %shard_map.37 = bf16[256,1024]{1,0:T(8,128)(2,1)S(1)} custom-call(bf16[256,1024]{1,0:T(8,128)(2,1)S(1)} %copy-done.1, bf16[3,128,1024]{2,1,0:T(8,128)(2,1)S(1)} %bitcast.2, f32[1,1024]{1,0:T(1,128)S(1)} %bitcast.3), custom_call_target="tpu_custom_call" | custom-call | tf_op jit(solution)/shard_map/pallas_call | solution.py:360
  97.5 0.8 copy.5
Async XLA Ops:
  0.0 1.1 %copy-start = (bf16[128,3,1024]{2,0,1:T(8,128)(2,1)S(1)}, bf16[128,3,1024]{2,0,1:T(8,128)(2,1)}, u32[]{:S(2)}) copy-start(bf16[128,3,1024]{2,0,1:T(8,128)(2,1)} %param.4) | copy-start | bytes 2359300
  1.1 1.0 %copy-start.1 = (bf16[256,1024]{1,0:T(8,128)(2,1)S(1)}, bf16[256,1024]{1,0:T(8,128)(2,1)}, u32[]{:S(2)}) copy-start(bf16[256,1024]{1,0:T(8,128)(2,1)} %x_ref.1) | copy-start | bytes 1572868
  2.2 0.7 copy-start.2

commit v2 on v0

v2 whole, which is shorter than its diff:
```python
import functools
import math

import jax
import jax.numpy as jnp
from jax import lax
from jax.experimental import pallas as pl
from jax.experimental.pallas import tpu as pltpu
from jax.sharding import PartitionSpec as P

HD = 128
GROUP = 4
BLOCK = 256

epsilon = 1e-06
MESH = pl.DeviceIdType.MESH
NN = (((1,), (0,)), ((), ()))
NT = (((1,), (1,)), ((), ()))
TN = (((0,), (0,)), ((), ()))


def split(x):
    high = x.astype(jnp.bfloat16)
    low = (x - high.astype(jnp.float32)).astype(jnp.bfloat16)
    return high, low


def dot(a, b, dims):
    one = functools.partial(
        lax.dot_general, dimension_numbers=dims, preferred_element_type=jnp.float32
    )
    return one(a[0], b[0]) + (one(a[0], b[1]) + one(a[1], b[0]))


def kernel(
    n, peers, group, x_ref, w_ref, gain_ref, out_ref,
    xbuf, wbuf, proj, ubuf, raw, s_own, s_in, r_own, r_in, result, landed,
    own_sem, slice_recv, slice_send, plane_recv, wup, wdown, xrecv, xsend, xcore,
    ssend, srecv, rsend, rrecv, osend, orecv,
):
    me, e = lax.axis_index("ctx"), lax.axis_index("head")
    t, h = me // group, me % group
    turns = n // group
    toks, feats = x_ref.shape
    rows = w_ref.shape[1]
    heads = wbuf.shape[0]
    width = heads * HD
    total = toks * group
    depth = rows * group
    order = (1, 0, 2)

    def ring(j):
        return (h + j) % group

    def other(o):
        return (e + o) % peers

    def at(tt, hh):
        return tt * group + hh

    barrier = pltpu.get_barrier_semaphore()
    for j in range(1, group):
        pl.semaphore_signal(barrier, inc=1, device_id=(at(t, ring(j)), e), device_id_type=MESH)
    for o in range(1, peers):
        pl.semaphore_signal(barrier, inc=1, device_id=(me, other(o)), device_id_type=MESH)

    @pl.loop(1, turns)
    def _(k):
        pl.semaphore_signal(
            barrier, inc=1, device_id=(at((t + k) % turns, h), e), device_id_type=MESH
        )

    pl.semaphore_wait(barrier, group - 1 + peers - 1 + turns - 1)

    def remote(src, dst, send, recv, to):
        return pltpu.make_async_remote_copy(
            src_ref=src, dst_ref=dst, send_sem=send, recv_sem=recv, device_id=to, device_id_type=MESH
        )

    def mcols(c):
        return slice(c * HD, (c + 1) * HD)

    def hcols(hh, i):
        return pl.ds(pl.multiple_of(hh * width + i * HD, HD), HD)

    def tok(hh):
        return pl.ds(pl.multiple_of(hh * toks, toks), toks)

    def kspan(ts):
        return pl.ds(pl.multiple_of(ts * depth, depth), depth)

    def slot(i, c, s):
        return wbuf.at[i, pl.ds(pl.multiple_of(s * rows, rows), rows), mcols(c)]

    def plane(i, c, ts):
        return wbuf.at[i, kspan(ts), mcols(c)]

    def across(i, c, j, s):
        hp = ring(j)
        return remote(
            w_ref.at[c, :, hcols(hp, i)], slot(i, c, s), slice_send.at[i, c, j],
            slice_recv.at[i, c, s % group], (at(t, hp), e),
        )

    def w_own(i, c):
        return pltpu.make_async_copy(w_ref.at[c, :, hcols(h, i)], slot(i, c, me), own_sem.at[i, c])

    def up(i, c, ts):
        p = plane(i, c, ts)
        return remote(p, p, wup.at[i, c, ts], plane_recv.at[i, c, ts], (at((t + 1) % turns, h), e))

    def down(i, c, ts):
        p = plane(i, c, ts)
        to = (at((t + turns - 1) % turns, h), e)
        return remote(p, p, wdown.at[i, c, ts], plane_recv.at[i, c, ts], to)

    def send_up(i, c, ts):
        @pl.when(t + 1 < turns)
        def _():
            up(i, c, ts).start()

    def send_down(i, c, ts):
        @pl.when(t > 0)
        def _():
            down(i, c, ts).start()

    def start_plane(i):
        for c in order:
            w_own(i, c).wait()
            for j in range(1, group):
                across(i, c, j, at(t, ring(j))).wait_recv()
            send_up(i, c, t)
            send_down(i, c, t)

    def arrive(i, d):
        for c in order:
            @pl.when(t - d >= 0)
            def _():
                up(i, c, t - d).wait_recv()
                send_up(i, c, t - d)

            @pl.when(t + d < turns)
            def _():
                down(i, c, t + d).wait_recv()
                send_down(i, c, t + d)

    def xslot(hh, ee):
        return xbuf.at[tok(hh), pl.ds(pl.multiple_of(ee * feats, feats), feats)]

    def xacross(j, hs):
        return remote(x_ref, xslot(hs, e), xsend.at[j], xrecv.at[hs, e], (at(t, ring(j)), e))

    def xsibling(j, o, ee):
        hs = ring(j)
        src = x_ref if j == 0 else xslot(hs, e)
        return remote(src, xslot(hs, ee), xcore.at[j, o], xrecv.at[hs, ee], (me, other(o)))

    x_own = pltpu.make_async_copy(x_ref, xslot(h, e), own_sem.at[heads, 0])

    def start_tokens():
        for j in range(1, group):
            xacross(j, h).start()
        for o in range(1, peers):
            xsibling(0, o, e).start()
        x_own.start()

    def finish_tokens():
        x_own.wait()
        for j in range(1, group):
            xacross(j, ring(j)).wait_recv()
            for o in range(1, peers):
                xsibling(j, o, e).start()
        for j in range(group):
            for o in range(1, peers):
                xsibling(j, o, other(o)).wait_recv()

    def multiply(i, ts, fresh):
        @pl.loop(0, group)
        def _(m):
            part = lax.dot_general(
                xbuf[tok(m), kspan(ts)], wbuf[i, kspan(ts), :], NN, preferred_element_type=jnp.float32
            )
            if fresh:
                proj[i, tok(m), :] = part
            else:
                proj[i, tok(m), :] += part

    def multiply_at(i, d):
        if d == 0:
            multiply(i, t, True)
            return

        @pl.when(t - d >= 0)
        def _():
            multiply(i, t - d, False)

        @pl.when(t + d < turns)
        def _():
            multiply(i, t + d, False)

    blk = math.gcd(total, BLOCK)
    blocks = total // blk
    causal = lax.broadcasted_iota(jnp.int32, (blk, blk), 0) >= lax.broadcasted_iota(
        jnp.int32, (blk, blk), 1
    )

    def over_blocks(f, first):
        if blocks > 4:
            return lax.fori_loop(0, blocks, f, first)
        for b in range(blocks):
            first = f(b, first)
        return first

    def span(b):
        return pl.ds(pl.multiple_of(b * blk, blk), blk)

    def part(i, c, b):
        return split(proj[i, span(b), mcols(c)])

    def push(own, into, send, recv, i, tp, ts):
        return remote(own.at[i], into.at[ts, i], send.at[i, tp], recv.at[i, ts], (at(tp, h), e))

    s_refs = (s_own, s_in, ssend, srecv)
    r_refs = (r_own, r_in, rsend, rrecv)
    zero = jnp.zeros((HD, HD), jnp.float32)

    def push_later(refs, i):
        @pl.loop(t + 1, turns)
        def _(tp):
            push(*refs, i, tp, t).start()

    def earlier(refs, i):
        def add(ts, sum_):
            push(*refs, i, (t + 1) % turns, ts).wait_recv()
            return sum_ + refs[1][ts, i]
        return lax.fori_loop(0, t, add, zero)

    def key_moments(i):
        def step(b, sum_):
            k = part(i, 1, b)
            return sum_ + dot(k, k, TN)
        s_own[i] = over_blocks(step, zero)
        push_later(s_refs, i)

    def local_keys(i):
        def step(b, sum_):
            q, k = part(i, 0, b), part(i, 1, b)
            scores = jnp.where(causal, dot(q, k, NT), 0.0)
            ubuf[i, span(b), :] = dot(split(scores), k, NN) + dot(q, split(sum_), NN)
            return sum_ + dot(k, k, TN)
        over_blocks(step, zero)

    def all_keys(i):
        before = split(earlier(s_refs, i))

        def step(b, sum_):
            u = ubuf[i, span(b), :] + dot(part(i, 0, b), before, NN)
            ubuf[i, span(b), :] = u
            return sum_ + dot(split(u), part(i, 2, b), TN)
        r_own[i] = over_blocks(step, zero)
        push_later(r_refs, i)

    def local_raw(i):
        def step(b, sum_):
            q, v, u = part(i, 0, b), part(i, 2, b), split(ubuf[i, span(b), :])
            scores = jnp.where(causal, dot(q, u, NT), 0.0)
            raw[i, span(b), :] = dot(split(scores), v, NN) + dot(q, split(sum_), NN)
            return sum_ + dot(u, v, TN)
        over_blocks(step, zero)

    def give(i, j, hh):
        hp = ring(j)
        return remote(
            result.at[i, tok(hp), :], landed.at[:, hcols(hh, i)], osend.at[i, j], orecv.at[i, hh],
            (at(t, hp), e),
        )

    def o_own(i):
        return pltpu.make_async_copy(
            result.at[i, tok(h), :], landed.at[:, hcols(h, i)], own_sem.at[heads, 1 + i]
        )

    def finish(i):
        before = split(earlier(r_refs, i))
        gain = gain_ref[:, hcols(h, i)]
        for j in list(range(1, group)) + [0]:
            rs = tok(ring(j))
            full = raw[i, rs, :] + dot(split(proj[i, rs, mcols(0)]), before, NN)
            mean_sq = jnp.mean(full * full, axis=-1, keepdims=True)
            result[i, rs, :] = (full * lax.rsqrt(mean_sq + epsilon) * gain).astype(jnp.bfloat16)
            (give(i, j, h) if j else o_own(i)).start()

    for i in range(heads):
        for c in order:
            w_own(i, c).start()
            for j in range(1, group):
                across(i, c, j, me).start()
    stages = (key_moments, local_keys, all_keys, local_raw, finish)
    if turns <= 8 and depth % 128 == 0:
        start_plane(0)
        start_tokens()
        for d in range(1, turns - 1):
            arrive(0, d)
        if heads > 1:
            start_plane(1)
        finish_tokens()
        for d in range(turns):
            if d == turns - 1 and d > 0:
                arrive(0, d)
            multiply_at(0, d)
        for i in range(heads):
            fill = []
            if i + 1 < heads:
                for d in range(turns):
                    if d + 1 < turns:
                        fill.append(functools.partial(arrive, i + 1, d + 1))
                    fill.append(functools.partial(multiply_at, i + 1, d))
            late = len(fill) - 4
            for stage in stages:
                stage(i)
                if len(fill) > late and len(fill) > 4:
                    fill.pop(0)()
                if stage is local_raw and i + 2 < heads:
                    start_plane(i + 2)
            for f in fill:
                f()
    else:
        start_tokens()
        for i in range(heads):
            start_plane(i)

            @pl.loop(1, turns)
            def _(d):
                arrive(i, d)
        finish_tokens()
        for i in range(heads):
            @pl.loop(0, group)
            def _(m):
                proj[i, tok(m), :] = lax.dot_general(
                    xbuf[tok(m), :], wbuf[i], NN, preferred_element_type=jnp.float32
                )
        for i in range(heads):
            for stage in stages:
                stage(i)

    for j in range(1, group):
        xacross(j, h).wait_send()
    for j in range(group):
        for o in range(1, peers):
            xsibling(j, o, e).wait_send()
    for i in range(heads):
        for c in order:
            for j in range(1, group):
                across(i, c, j, me).wait_send()

            @pl.when(t + 1 < turns)
            def _():
                @pl.loop(0, t + 1)
                def _(ts):
                    up(i, c, ts).wait_send()

            @pl.when(t > 0)
            def _():
                @pl.loop(t, turns)
                def _(ts):
                    down(i, c, ts).wait_send()

        @pl.loop(t + 1, turns)
        def _(tp):
            push(*s_refs, i, tp, t).wait_send()
            push(*r_refs, i, tp, t).wait_send()

        o_own(i).wait()
        for j in range(1, group):
            give(i, j, h).wait_send()
            give(i, j, ring(j)).wait_recv()
    out_ref[...] = landed[...]


def body(tokens, qkv_weight, out_gain):
    n, peers = lax.axis_size("ctx"), lax.axis_size("head")
    toks, feats = tokens.shape
    rows, _, cols = qkv_weight.shape
    group = math.gcd(math.gcd(n, cols // HD), GROUP)
    turns = n // group
    width = cols // group
    heads = width // HD
    total = toks * group
    moments = (heads, HD, HD)
    f32, bf16 = jnp.float32, jnp.bfloat16
    dma = pltpu.SemaphoreType.DMA
    vmem = pl.BlockSpec(memory_space=pltpu.VMEM)
    return pl.pallas_call(
        functools.partial(kernel, n, peers, group),
        out_shape=jax.ShapeDtypeStruct((toks, cols), bf16),
        in_specs=[pl.BlockSpec(memory_space=pl.ANY)] * 2 + [vmem],
        out_specs=vmem,
        scratch_shapes=[
            pltpu.VMEM((total, feats * peers), bf16),
            pltpu.VMEM((heads, rows * n, 3 * HD), bf16),
            pltpu.VMEM((heads, total, 3 * HD), f32),
            pltpu.VMEM((heads, total, HD), f32),
            pltpu.VMEM((heads, total, HD), f32),
            pltpu.VMEM(moments, f32),
            pltpu.VMEM((turns,) + moments, f32),
            pltpu.VMEM(moments, f32),
            pltpu.VMEM((turns,) + moments, f32),
            pltpu.VMEM((heads, total, HD), bf16),
            pltpu.VMEM((toks, cols), bf16),
            dma((heads + 1, max(3, heads + 1))),
            dma((heads, 3, group)),
            dma((heads, 3, group)),
            dma((heads, 3, turns)),
            dma((heads, 3, turns)),
            dma((heads, 3, turns)),
            dma((group, peers)),
            dma((group,)),
            dma((group, peers)),
            dma((heads, turns)),
            dma((heads, turns)),
            dma((heads, turns)),
            dma((heads, turns)),
            dma((heads, group)),
            dma((heads, group)),
        ],
        compiler_params=pltpu.CompilerParams(
            collective_id=0, has_side_effects=True, vmem_limit_bytes=48 * 1024 * 1024
        ),
    )(tokens, qkv_weight.transpose(1, 0, 2), out_gain.reshape(1, cols))


def solution(mesh):
    in_specs = (P("ctx", "head"), P("ctx", None, "head"), P("head"))
    out_specs = P("ctx", "head")
    return jax.shard_map(body, mesh=mesh, in_specs=in_specs, out_specs=out_specs, check_vma=False)
```

time: 669 us -> 90.4 us (0.14)
  waiting for transfers between devices: 533 us -> 0 us
  Pallas kernels: 0 us -> 86.5 us
  matrix products: 46.9 us -> 0 us
  other arithmetic: 46 us -> 0 us
  local copies, waits for them, and re-layouts: 23.7 us -> 3.66 us
  between operations: 13.4 us -> 0.01 us
    all_gather x5 -> x0, waiting for transfers between devices: 532 us -> none  [the longest x3 324 us: prefix(): everything = jax.tree.map(lambda part: lax.all_gather(part, axis), x)]
    pallas_call x0 -> x1, Pallas kernels: none -> 86.5 us  [body(): pl.pallas_call(functools.partial(kernel, n, peers, group), out_shape=jax....]
    dot_general x32 -> x0, matrix products: 46.9 us -> none  [the longest x1 6.89 us: body(): jnp.einsum('tr,rch->cth', gathered, lax.all_gather(qkv_weight, 'ctx', axi...]
    select_n x32 -> x0, other arithmetic: 44.7 us -> none  [step(): return jax.tree.map(lambda a, b: jnp.where(reached, a, b), new, before)]
    dynamic_slice x4 -> x0, local copies, waits for them, and re-layouts: 8.8 us -> none  [body(): lax.scan(local_step, (zeros_state, zeros_state, zeros_state), (queries, k...]
    squeeze x4 -> x0, local copies, waits for them, and re-layouts: 8.24 us -> none  [the longest x2 4.01 us: body(): queries = projected[0]]
  transfers between devices with their start and end apart: 5 -> 0, of which waited for: 5 -> 0; matrix products, arithmetic and copies ran while one was open for 2% -> 0% of each run, Pallas kernels for 0% -> 0%
where the time goes in v2:
time: 90.4 us; the launch traced here: 90.2 us
  Pallas kernels  86.5 us (96%)
  local copies, waits for them, and re-layouts  3.66 us (4%)
    pallas_call x1, Pallas kernels, body(): pl.pallas_call(functools.partial(kernel, n, peers, group), out_shape=jax....  86.5 us
    unnamed x7, local copies, waits for them, and re-layouts  3.66 us

profile of v2, /device:TPU:25, one launch (start us, length us, event | category | flops | bytes accessed | tf_op | source)
XLA Modules:
  0.0 90.2 jit_solution(8368389034796119193)
XLA Ops:
  0.0 0.0 copy-start
  0.0 1.1 %copy-done = bf16[128,3,1024]{2,0,1:T(8,128)(2,1)S(1)} copy-done((bf16[128,3,1024]{2,0,1:T(8,128)(2,1)S(1)}, bf16[128,3,1024]{2,0,1:T(8,128)(2,1)}, u32[]{:S(2)}) %copy-start) | copy-done | bytes 786456
  1.1 0.0 copy-start.1
  1.1 1.0 %copy-done.1 = bf16[256,1024]{1,0:T(8,128)(2,1)S(1)} copy-done((bf16[256,1024]{1,0:T(8,128)(2,1)S(1)}, bf16[256,1024]{1,0:T(8,128)(2,1)}, u32[]{:S(2)}) %copy-start.1) | copy-done | bytes 524312
  2.2 0.0 copy-start.2
  2.2 0.7 copy-done.2
  2.9 86.5 %shard_map.37 = bf16[256,1024]{1,0:T(8,128)(2,1)S(1)} custom-call(bf16[256,1024]{1,0:T(8,128)(2,1)S(1)} %copy-done.1, bf16[3,128,1024]{2,1,0:T(8,128)(2,1)S(1)} %bitcast.2, f32[1,1024]{1,0:T(1,128)S(1)} %bitcast.3), custom_call_target="tpu_custom_call" | custom-call | tf_op jit(solution)/shard_map/pallas_call | solution.py:393
  89.4 0.8 copy.5
Async XLA Ops:
  0.0 1.1 %copy-start = (bf16[128,3,1024]{2,0,1:T(8,128)(2,1)S(1)}, bf16[128,3,1024]{2,0,1:T(8,128)(2,1)}, u32[]{:S(2)}) copy-start(bf16[128,3,1024]{2,0,1:T(8,128)(2,1)} %param.4) | copy-start | bytes 2359300
  1.1 1.0 %copy-start.1 = (bf16[256,1024]{1,0:T(8,128)(2,1)S(1)}, bf16[256,1024]{1,0:T(8,128)(2,1)}, u32[]{:S(2)}) copy-start(bf16[256,1024]{1,0:T(8,128)(2,1)} %x_ref.1) | copy-start | bytes 1572868
  2.2 0.7 copy-start.2

commit v3 on v2

--- a/solution.py
+++ b/solution.py
@@ -225,15 +225,23 @@
     zero = jnp.zeros((HD, HD), jnp.float32)
 
     def push_later(refs, i):
-        @pl.loop(t + 1, turns)
-        def _(tp):
-            push(*refs, i, tp, t).start()
+        @pl.when((t == 0) & (turns > 1))
+        def _():
+            push(*refs, i, 1, t).start()
 
     def earlier(refs, i):
         def add(ts, sum_):
             push(*refs, i, (t + 1) % turns, ts).wait_recv()
             return sum_ + refs[1][ts, i]
-        return lax.fori_loop(0, t, add, zero)
+
+        sum_ = lax.fori_loop(jnp.maximum(t - 1, 0), t, add, zero)
+
+        @pl.when((t > 0) & (t + 1 < turns))
+        def _():
+            refs[0][i] += sum_
+            push(*refs, i, t + 1, t).start()
+
+        return sum_
 
     def key_moments(i):
         def step(b, sum_):
@@ -365,10 +373,10 @@
                 def _(ts):
                     down(i, c, ts).wait_send()
 
-        @pl.loop(t + 1, turns)
-        def _(tp):
-            push(*s_refs, i, tp, t).wait_send()
-            push(*r_refs, i, tp, t).wait_send()
+        @pl.when(t + 1 < turns)
+        def _():
+            push(*s_refs, i, t + 1, t).wait_send()
+            push(*r_refs, i, t + 1, t).wait_send()
 
         o_own(i).wait()
         for j in range(1, group):

time: 90.4 us -> 88.1 us (0.975)
  Pallas kernels: 86.5 us -> 84.2 us
    pallas_call x1, Pallas kernels: 86.5 us -> 84.2 us  [body(): pl.pallas_call(functools.partial(kernel, n, peers, group), out_shape=jax....]
where the time goes in v3:
time: 88.1 us; the launch traced here: 87.9 us
  Pallas kernels  84.2 us (96%)
  local copies, waits for them, and re-layouts  3.66 us (4%)
    pallas_call x1, Pallas kernels, body(): pl.pallas_call(functools.partial(kernel, n, peers, group), out_shape=jax....  84.2 us
    unnamed x7, local copies, waits for them, and re-layouts  3.66 us

profile of v3, /device:TPU:25, one launch (start us, length us, event | category | flops | bytes accessed | tf_op | source)
XLA Modules:
  0.0 87.9 jit_solution(12921524191010677291)
XLA Ops:
  0.0 0.0 copy-start
  0.0 1.1 %copy-done = bf16[128,3,1024]{2,0,1:T(8,128)(2,1)S(1)} copy-done((bf16[128,3,1024]{2,0,1:T(8,128)(2,1)S(1)}, bf16[128,3,1024]{2,0,1:T(8,128)(2,1)}, u32[]{:S(2)}) %copy-start) | copy-done | bytes 786456
  1.1 0.0 copy-start.1
  1.1 1.0 %copy-done.1 = bf16[256,1024]{1,0:T(8,128)(2,1)S(1)} copy-done((bf16[256,1024]{1,0:T(8,128)(2,1)S(1)}, bf16[256,1024]{1,0:T(8,128)(2,1)}, u32[]{:S(2)}) %copy-start.1) | copy-done | bytes 524312
  2.2 0.0 copy-start.2
  2.2 0.7 copy-done.2
  2.9 84.2 %shard_map.37 = bf16[256,1024]{1,0:T(8,128)(2,1)S(1)} custom-call(bf16[256,1024]{1,0:T(8,128)(2,1)S(1)} %copy-done.1, bf16[3,128,1024]{2,1,0:T(8,128)(2,1)S(1)} %bitcast.2, f32[1,1024]{1,0:T(1,128)S(1)} %bitcast.3), custom_call_target="tpu_custom_call" | custom-call | tf_op jit(solution)/shard_map/pallas_call | solution.py:401
  87.1 0.8 copy.5
Async XLA Ops:
  0.0 1.1 %copy-start = (bf16[128,3,1024]{2,0,1:T(8,128)(2,1)S(1)}, bf16[128,3,1024]{2,0,1:T(8,128)(2,1)}, u32[]{:S(2)}) copy-start(bf16[128,3,1024]{2,0,1:T(8,128)(2,1)} %param.4) | copy-start | bytes 2359300
  1.1 1.0 %copy-start.1 = (bf16[256,1024]{1,0:T(8,128)(2,1)S(1)}, bf16[256,1024]{1,0:T(8,128)(2,1)}, u32[]{:S(2)}) copy-start(bf16[256,1024]{1,0:T(8,128)(2,1)} %x_ref.1) | copy-start | bytes 1572868
  2.2 0.7 copy-start.2
